TPU v7x, 128 devices: a whole 4x4x4 slice. The times are simulated.
128 devices in a mesh: attn: 8 (over z, core), expert: 16 (over x, y).
Axes of the slice: x: 4, y: 4, z: 4, core: 2. Of those that a mesh axis runs over, the one named last changes fastest.
Arguments:
- queries: bfloat16 [32, 64, 576], P('attn'), may hold values from -11 to 11
- cache: bfloat16 [24576, 64, 576], P(('attn', 'expert')), may hold values from -6 to 6
- owner: int32 [24576], P(('attn', 'expert')), may hold values from 0 to 4, as said below
- uv_weight: bfloat16 [64, 512, 128], P('expert'), may hold values from -0.25 to 0.25
- out_weight: bfloat16 [8192, 7168], P('expert')
- norm_gain: float32 [7168], replicated, may hold values from 0.1 to 1.9
- expert_ids: int32 [32, 8], P('attn'), may hold values from 0 to 15, all different within a row; in each aligned block of 4 rows (0 to 3, 4 to 7, ...) at most 4 rows name the same one
- gate_values: float32 [32, 8], P('attn'), may hold values from 0.1 to 1
- gate_weight: bfloat16 [16, 7168, 2048], P('attn', None, 'expert'), may hold values from -0.0625 to 0.0625
- up_weight: bfloat16 [16, 7168, 2048], P('attn', None, 'expert'), may hold values from -0.0625 to 0.0625
- down_weight: bfloat16 [16, 2048, 7168], P('attn', 'expert'), may hold values from -0.1875 to 0.1875
Outputs:
- layer_out: bfloat16 [32, 7168], P('attn', 'expert')
Inputs may be any that keep to these rules, and one draw needn't show every extreme that they name: owner[p] names one of the 4 requests of page p's attention index, or is 4 for an empty slot; every request holds at least one page. `expert_ids`: among the rows of one attention index, no expert is named by more than 4 rows.
All inputs are finite; a program needn't handle non-finite values.
Results may differ from a plain program's by a relative error of at most 0.035.
Values may be sent and summed in bfloat16 or wider, within the bound.
A program may use at most 192 MiB of HBM per device.

v0:
```python
import jax
import jax.numpy as jnp
from jax import lax
from jax.sharding import PartitionSpec as P

NEGATIVE = -1e30
SCORE_SCALE = 192.0 ** (-0.5)
EPSILON = 1e-06
HIGHEST = lax.Precision.HIGHEST


def local_attention(queries, cache, owner, latent_width):
    row_count = queries.shape[0]
    head_count = queries.shape[1]
    pool_size = cache.shape[0]
    valid_pages = owner < row_count
    safe_owner = jnp.minimum(owner, row_count - 1)
    picked = jnp.take(queries, safe_owner, axis=0)
    scores = (
        jnp.einsum("phc,ptc->pht", picked, cache, preferred_element_type=jnp.float32) * SCORE_SCALE
    )
    page_max = jnp.where(valid_pages[:, None], jnp.max(scores, axis=2), NEGATIVE)
    member = (safe_owner[:, None] == jnp.arange(row_count, dtype=jnp.int32)[None, :]) & valid_pages[
        :, None
    ]
    row_max = jnp.max(jnp.where(member[:, :, None], page_max[:, None, :], NEGATIVE), axis=0)
    weights = jnp.where(
        valid_pages[:, None, None],
        jnp.exp(scores - jnp.take(row_max, safe_owner, axis=0)[:, :, None]),
        0.0,
    )
    probs = weights.astype(jnp.bfloat16)
    page_sum = jnp.einsum(
        "pht,ptc->phc", probs, cache[:, :, :latent_width], preferred_element_type=jnp.float32
    )
    member_float = member.astype(jnp.float32)
    totals = jnp.dot(member_float.T, jnp.sum(weights, axis=2), precision=HIGHEST)
    summed = jnp.dot(member_float.T, page_sum.reshape(pool_size, -1), precision=HIGHEST)
    return (row_max, totals, summed.reshape(row_count, head_count, latent_width))


def expert_work(arriving, gate_weight, up_weight, down_weight):
    gate_proj = jnp.einsum(
        "sjcd,jdf->sjcf", arriving, gate_weight, preferred_element_type=jnp.float32
    )
    up_proj = jnp.einsum("sjcd,jdf->sjcf", arriving, up_weight, preferred_element_type=jnp.float32)
    hidden = (jax.nn.silu(gate_proj) * up_proj).astype(jnp.bfloat16)
    return jnp.einsum("sjcf,jfd->sjcd", hidden, down_weight, preferred_element_type=jnp.float32)


def round_trip(slot_block, share_map, gate_weight, up_weight, down_weight):
    arriving = lax.all_to_all(slot_block, "attn", split_axis=0, concat_axis=0, tiled=True)
    produced = expert_work(arriving, gate_weight, up_weight, down_weight)
    reduced = lax.psum_scatter(produced, "expert", scatter_dimension=3, tiled=True)
    returned = lax.all_to_all(reduced, "attn", split_axis=0, concat_axis=0, tiled=True)
    flattened = returned.reshape(-1, returned.shape[3])
    return jnp.einsum("sr,sd->rd", share_map, flattened, precision=HIGHEST)


def on_device(
    queries,
    cache,
    owner,
    uv_weight,
    out_weight,
    norm_gain,
    expert_ids,
    gate_values,
    gate_weight,
    up_weight,
    down_weight,
):
    row_count = queries.shape[0]
    latent_width = uv_weight.shape[1]
    row_max, totals, summed = local_attention(queries, cache, owner, latent_width)
    maxima, denominators, numerators = (
        lax.all_to_all(row_max[None], "expert", split_axis=2, concat_axis=0, tiled=True),
        lax.all_to_all(totals[None], "expert", split_axis=2, concat_axis=0, tiled=True),
        lax.all_to_all(summed[None], "expert", split_axis=2, concat_axis=0, tiled=True),
    )
    peaks = jnp.max(maxima, axis=0)
    rescale = jnp.exp(maxima - peaks[None])
    total_weight = jnp.sum(rescale * denominators, axis=0)
    attended = (
        jnp.sum(rescale[:, :, :, None] * numerators, axis=0) / total_weight[:, :, None]
    ).astype(jnp.bfloat16)
    mixed_heads = jnp.einsum(
        "rhc,hcv->rhv", attended, uv_weight, preferred_element_type=jnp.float32
    )
    mixed_heads = mixed_heads.astype(jnp.bfloat16).reshape(row_count, -1)
    partial_out = jnp.dot(mixed_heads, out_weight, preferred_element_type=jnp.float32)
    attn_out = lax.psum(partial_out, "expert")
    mean_square = jnp.mean(attn_out * attn_out, axis=1, keepdims=True)
    normed = (attn_out * lax.rsqrt(mean_square + EPSILON) * norm_gain[None, :]).astype(jnp.bfloat16)
    attn_size = lax.axis_size("attn")
    expert_size = lax.axis_size("expert")
    local_experts = gate_weight.shape[0]
    expert_total = local_experts * attn_size
    top_count = expert_ids.shape[1]
    model_width = normed.shape[1]
    capacity = min(
        row_count, 2 * ((3 * row_count * top_count + 4 * expert_total - 1) // (4 * expert_total))
    )
    flat_ids = expert_ids.reshape(-1)
    matches = (flat_ids[:, None] == jnp.arange(expert_total, dtype=jnp.int32)[None, :]).astype(
        jnp.int32
    )
    earlier = jnp.cumsum(matches, axis=0) - matches
    position = jnp.sum(earlier * matches, axis=1)
    slot_index = (flat_ids * capacity + position).reshape(row_count, top_count)
    chosen = (
        jnp.arange(expert_total * capacity, dtype=jnp.int32)[:, None, None]
        == slot_index[None, :, :]
    )
    pick_map = jnp.any(chosen, axis=2).astype(jnp.bfloat16)
    weight_map = jnp.sum(jnp.where(chosen, gate_values[None, :, :], 0.0), axis=2)
    outgoing = jnp.dot(pick_map, normed, preferred_element_type=jnp.float32).astype(jnp.bfloat16)
    outgoing = outgoing.reshape(attn_size, local_experts, capacity, model_width)
    weight_grid = weight_map.reshape(attn_size, local_experts, capacity, row_count)
    share_map = weight_grid.reshape(-1, row_count)
    section_sum = round_trip(outgoing, share_map, gate_weight, up_weight, down_weight)
    column_width = model_width // expert_size
    attn_columns = lax.dynamic_slice_in_dim(
        attn_out, lax.axis_index("expert") * column_width, column_width, 1
    )
    return (attn_columns + section_sum).astype(jnp.bfloat16)


def solution(mesh):
    placed = (
        P("attn", None, None),
        P(("attn", "expert"), None, None),
        P(("attn", "expert")),
        P("expert", None, None),
        P("expert", None),
        P(),
        P("attn", None),
        P("attn", None),
        P("attn", None, "expert"),
        P("attn", None, "expert"),
        P("attn", "expert", None),
    )
    return jax.shard_map(
        on_device, mesh=mesh, in_specs=placed, out_specs=P("attn", "expert"), check_vma=False
    )
```

profile of v0, /device:TPU:1, one launch (start us, length us, event | category | flops | bytes accessed | tf_op | source)
XLA Modules:
  0.0 384.2 jit_solution(11106621884005514824)
XLA Ops:
  6.5 0.7 broadcast_minimum_fusion
  7.3 0.7 broadcast_compare_fusion
  8.0 10.3 %gather_fusion = bf16[192,64,576]{2,1,0:T(8,128)(2,1)} fusion(bf16[4,64,576]{2,1,0:T(8,128)(2,1)} %param.11, s32[1024]{0:T(1024)S(1)} %pad_clamp_fusion), kind=kCustom, calls=%fused_computation | custom fusion | bytes 28312320 | tf_op jit(solution)/shard_map/jit(_take)/gather | solution.py:18
  18.3 15.5 %fusion.3 = f32[192,64,64]{1,2,0:T(8,128)} fusion(bf16[192,64,576]{2,1,0:T(8,128)(2,1)} %param.12, bf16[192,64,576]{2,1,0:T(8,128)(2,1)} %gather_fusion, pred[192]{0:T(512)(128)(4,1)S(1)} %get-tuple-element.12), kind=kOutput, calls=%fused_computation.5 | convolution fusion | flops 913047552 | bytes 31457472 | tf_op jit(solution)/shard_map/phc,ptc->pht/dot_general | solution.py:20
  33.7 7.6 %copy.80 = f32[192,64,64]{0,2,1:T(8,128)} copy(f32[192,64,64]{1,2,0:T(8,128)} %fusion.3) | data formatting | bytes 6291456 | tf_op jit(solution)/shard_map/phc,ptc->pht/dot_general | solution.py:20
  41.3 2.9 multiply_reduce_fusion
  44.6 0.7 gather_fusion.1
  45.5 3.5 fusion.14
  49.0 0.8 fusion.43
  49.7 7.6 %all-to-all-start.2 = ((f32[1,4,64]{1,0,2:T(1,128)}), f32[1,4,64]{1,0,2:T(1,128)S(1)}, u32[]{:S(2)}, u32[]{:S(2)}) async-start(f32[1,4,64]{1,0,2:T(1,128)} %bitcast.38), calls=%async_computation.2 | async-start | bytes 65536 | tf_op jit(solution)/shard_map/all_to_all | solution.py:78
  57.3 3.8 copy.87
  61.1 17.2 %fusion.6 = f32[192,64,512]{2,1,0:T(8,128)} fusion(bf16[192,64,64]{2,1,0:T(8,128)(2,1)} %copy.87, bf16[192,64,576]{2,1,0:T(8,128)(2,1)} %param.12), kind=kOutput, calls=%fused_computation.8 | convolution fusion | flops 805306368 | bytes 40894464 | tf_op jit(solution)/shard_map/pht,ptc->phc/dot_general | solution.py:33
  78.4 0.7 copy.83
  79.1 6.7 %all-to-all-start = ((f32[1,4,64]{1,0,2:T(1,128)}), f32[1,4,64]{1,0,2:T(1,128)S(1)}, u32[]{:S(2)}, u32[]{:S(2)}) async-start(f32[1,4,64]{1,0,2:T(1,128)} %copy.83), calls=%async_computation | async-start | bytes 65536 | tf_op jit(solution)/shard_map/all_to_all | solution.py:77
  85.8 28.2 %fusion.16 = f32[1,4,64,512]{3,1,0,2:T(4,128)} fusion(pred[192,4]{0,1:T(4,128)(4,1)S(1)} %fusion.38, f32[24,8,64,512]{3,2,1,0:T(8,128)} %bitcast.99), kind=kOutput, calls=%fused_computation.22 | convolution fusion | flops 301989888 | bytes 25690880 | tf_op jit(solution)/shard_map/dot_general | solution.py:38
  114.1 6.7 %all-to-all-start.1 = ((f32[1,4,64,512]{3,1,0,2:T(4,128)}), f32[1,4,64,512]{3,1,0,2:T(4,128)S(1)}, u32[]{:S(2)}, u32[]{:S(2)}) async-start(f32[1,4,64,512]{3,1,0,2:T(4,128)} %fusion.16), calls=%async_computation.1 | async-start | bytes 1048576 | tf_op jit(solution)/shard_map/all_to_all | solution.py:79
  122.2 7.8 %all-to-all-done.1 = f32[1,4,64,512]{3,1,0,2:T(4,128)S(1)} async-done(((f32[1,4,64,512]{3,1,0,2:T(4,128)}), f32[1,4,64,512]{3,1,0,2:T(4,128)S(1)}, u32[]{:S(2)}, u32[]{:S(2)}) %all-to-all-start.1) | async-done | bytes 524320 | tf_op jit(solution)/shard_map/all_to_all | solution.py:79
  130.2 5.0 %fusion.23 = f32[4,7168]{1,0:T(4,128)} fusion(bf16[512,7168]{1,0:T(8,128)(2,1)} %param.15, bf16[4,512,128]{2,1,0:T(8,128)(2,1)S(1)} %copy-done, f32[4,4,512]{2,0,1:T(4,128)S(1)} %multiply_reduce_fusion.1, f32[4,4]{0,1:T(4,128)S(1)} %copy.92), kind=kOutput, calls=%fused_computation.29 | convolution fusion | flops 31475712 | bytes 8011840 | tf_op jit(solution)/shard_map/dot_general | solution.py:91
  135.3 81.5 %all-reduce.2.cloned.1.call-done = f32[4,7168]{1,0:T(4,128)} async-done(((f32[4,7168]{1,0:T(4,128)}), f32[4,7168]{1,0:T(4,128)}) %all-reduce.2.cloned.1.call-update) | async-done | bytes 114704 | tf_op jit(solution)/shard_map/psum | solution.py:92
  216.8 1.1 multiply_reduce_fusion.2
  217.9 1.4 convolution_convert_fusion
  219.6 20.8 %all_to_all.64 = bf16[8,2,4,7168]{3,2,1,0:T(4,128)(2,1)S(1)} all-to-all(bf16[8,2,4,7168]{3,2,1,0:T(4,128)(2,1)S(1)} %reshape.116), channel_id=1, replica_groups=mesh['attn'=8,'expert'=16] {'attn'}, dimensions={0} | all-to-all | bytes 1835008 | tf_op jit(solution)/shard_map/all_to_all | solution.py:52
  240.4 3.0 fusion.10
  243.4 0.8 fusion.12
  244.8 18.9 %copy.103 = f32[8,2,4,7168]{0,2,1,3:T(4,128)} copy(f32[8,2,4,7168]{3,0,2,1:T(8,128)S(1)} %convolution_bitcast_fusion) | data formatting | bytes 3670016
  263.8 24.2 %reshape.140 = f32[7168,64]{1,0:T(8,128)} reshape(f32[7168,2,4,8]{3,2,1,0:T(4,128)} %bitcast.100) | data formatting | bytes 3670016
  288.0 72.0 %reduce-scatter.4.cloned.1.call-done = f32[448,64]{1,0:T(8,128)} async-done(((f32[7168,64]{1,0:T(8,128)}), f32[448,64]{1,0:T(8,128)}) %reduce-scatter.4.cloned.1.call-update) | async-done | bytes 114704
  360.0 2.2 reshape.141
  362.2 1.6 copy.97
  363.7 6.8 %all-to-all-start.4 = ((f32[8,2,4,448]{3,2,1,0:T(4,128)}), f32[8,2,4,448]{3,2,1,0:T(4,128)S(1)}, u32[]{:S(2)}, u32[]{:S(2)}) async-start(f32[8,2,4,448]{3,2,1,0:T(4,128)} %copy.97), calls=%async_computation.4 | async-start | bytes 262144 | tf_op jit(solution)/shard_map/all_to_all | solution.py:55
  370.6 5.2 %all-to-all-done.4 = f32[8,2,4,448]{3,2,1,0:T(4,128)S(1)} async-done(((f32[8,2,4,448]{3,2,1,0:T(4,128)}), f32[8,2,4,448]{3,2,1,0:T(4,128)S(1)}, u32[]{:S(2)}, u32[]{:S(2)}) %all-to-all-start.4) | async-done | bytes 114720 | tf_op jit(solution)/shard_map/all_to_all | solution.py:55
  375.9 1.5 fusion.19
  (45 shorter events, 3.5 us)
Async XLA Ops:
  6.5 123.6 %copy-start = (bf16[4,512,128]{2,1,0:T(8,128)(2,1)S(1)}, bf16[4,512,128]{2,1,0:T(8,128)(2,1)}, u32[]{:S(2)}) copy-start(bf16[4,512,128]{2,1,0:T(8,128)(2,1)} %param.14) | copy-start | bytes 1572868
  49.7 29.3 %all-to-all-start.2 = ((f32[1,4,64]{1,0,2:T(1,128)}), f32[1,4,64]{1,0,2:T(1,128)S(1)}, u32[]{:S(2)}, u32[]{:S(2)}) async-start(f32[1,4,64]{1,0,2:T(1,128)} %bitcast.38), calls=%async_computation.2 | async-start | bytes 65536 | tf_op jit(solution)/shard_map/all_to_all | solution.py:78
  79.1 35.0 %all-to-all-start = ((f32[1,4,64]{1,0,2:T(1,128)}), f32[1,4,64]{1,0,2:T(1,128)S(1)}, u32[]{:S(2)}, u32[]{:S(2)}) async-start(f32[1,4,64]{1,0,2:T(1,128)} %copy.83), calls=%async_computation | async-start | bytes 65536 | tf_op jit(solution)/shard_map/all_to_all | solution.py:77
  85.7 28.3 %copy-start.3 = (s32[4,8]{1,0:T(4,128)S(1)}, s32[4,8]{1,0:T(4,128)}, u32[]{:S(2)}) copy-start(s32[4,8]{1,0:T(4,128)} %param.17) | copy-start | bytes 388
  114.1 15.9 %all-to-all-start.1 = ((f32[1,4,64,512]{3,1,0,2:T(4,128)}), f32[1,4,64,512]{3,1,0,2:T(4,128)S(1)}, u32[]{:S(2)}, u32[]{:S(2)}) async-start(f32[1,4,64,512]{3,1,0,2:T(4,128)} %fusion.16), calls=%async_computation.1 | async-start | bytes 1048576 | tf_op jit(solution)/shard_map/all_to_all | solution.py:79
  120.8 96.0 %all-reduce.2.cloned.1.call-start = ((), (), s32[]{:S(2)}) async-start(), calls=%async_computation.6 | async-start | bytes 229376 | tf_op jit(solution)/shard_map/psum | solution.py:92
  130.2 87.7 %copy-start.2 = (f32[7168]{0:T(1024)S(1)}, f32[7168]{0:T(1024)}, u32[]{:S(2)}) copy-start(f32[7168]{0:T(1024)} %param.16) | copy-start | bytes 86020
  135.2 224.8 %reduce-scatter.4.cloned.1.call-start = ((), (), s32[]{:S(2)}) async-start(), calls=%async_computation.7 | async-start | bytes 3899392
  219.6 23.8 %copy-start.5 = (bf16[2,7168,128]{2,1,0:T(8,128)(2,1)S(1)}, bf16[2,7168,128]{2,1,0:T(8,128)(2,1)}, u32[]{:S(2)}) copy-start(bf16[2,7168,128]{2,1,0:T(8,128)(2,1)} %param.19) | copy-start | bytes 11010052
  240.4 3.8 copy-start.1
  288.0 82.6 %copy-start.4 = (f32[4,8]{1,0:T(4,128)S(1)}, f32[4,8]{1,0:T(4,128)}, u32[]{:S(2)}) copy-start(f32[4,8]{1,0:T(4,128)} %param.18) | copy-start | bytes 388
  363.7 12.1 %all-to-all-start.4 = ((f32[8,2,4,448]{3,2,1,0:T(4,128)}), f32[8,2,4,448]{3,2,1,0:T(4,128)S(1)}, u32[]{:S(2)}, u32[]{:S(2)}) async-start(f32[8,2,4,448]{3,2,1,0:T(4,128)} %copy.97), calls=%async_computation.4 | async-start | bytes 262144 | tf_op jit(solution)/shard_map/all_to_all | solution.py:55
Sparse Core Ops, SparseCore 0:
  135.3 81.4 all-reduce.1
  288.1 71.8 reduce-scatter.3
where the time goes:
time: 385 us; the launch traced here: 384 us
  waiting for transfers between devices  166 us (43%)
  matrix products  73.9 us (19%)
  local copies, waits for them, and re-layouts  71.5 us (19%)
  starting transfers between devices  28 us (7%)
  blocking collectives  20.8 us (5%)
  between operations  13.6 us (4%)
  other arithmetic  9.93 us (3%)
    psum x1, waiting for transfers between devices, on_device(): attn_out = lax.psum(partial_out, 'expert')  81.5 us
    unnamed x3, waiting for transfers between devices  72 us
    unnamed x16, local copies, waits for them, and re-layouts  45.4 us
    dot_general x1, matrix products, local_attention(): jnp.dot(member_float.T, page_sum.reshape(pool_size, -1), precision=HIGHEST)  28.2 us
    all_to_all x1, blocking collectives, round_trip(): lax.all_to_all(slot_block, 'attn', split_axis=0, concat_axis=0, tiled=True)  20.8 us
    dot_general x1, matrix products, local_attention(): jnp.einsum('pht,ptc->phc', probs, cache[:, :, :latent_width], preferred_e...  17.2 us
    dot_general x1, matrix products, local_attention(): jnp.einsum('phc,ptc->pht', picked, cache, preferred_element_type=jnp.floa...  15.5 us
    gather x1, local copies, waits for them, and re-layouts, local_attention(): picked = jnp.take(queries, safe_owner, axis=0)  10.3 us
  transfers between devices with their start and end apart: 6, of which 4 were waited for; matrix products, arithmetic and copies ran while one was open for 13% of the time, Pallas kernels for 0%

commit v1 on v0

--- a/solution.py
+++ b/solution.py
@@ -89,7 +89,11 @@
     )
     mixed_heads = mixed_heads.astype(jnp.bfloat16).reshape(row_count, -1)
     partial_out = jnp.dot(mixed_heads, out_weight, preferred_element_type=jnp.float32)
-    attn_out = lax.psum(partial_out, "expert")
+    attn_out = partial_out
+    for hop in (1, 2, 4, 8):
+        attn_out = attn_out + lax.ppermute(
+            attn_out, "expert", [(dev, dev ^ hop) for dev in range(16)]
+        )
     mean_square = jnp.mean(attn_out * attn_out, axis=1, keepdims=True)
     normed = (attn_out * lax.rsqrt(mean_square + EPSILON) * norm_gain[None, :]).astype(jnp.bfloat16)
     attn_size = lax.axis_size("attn")

time: 385 us -> 324 us (0.84)
  waiting for transfers between devices: 166 us -> 99.3 us
  blocking collectives: 20.8 us -> 27.7 us
    psum x1 -> x0, waiting for transfers between devices: 81.5 us -> none  [on_device(): attn_out = lax.psum(partial_out, 'expert')]
    ppermute x0 -> x4, waiting for transfers between devices: none -> 14.9 us  [on_device(): lax.ppermute(attn_out, 'expert', [(dev, dev ^ hop) for dev in range(16)])]
    all_to_all x1, blocking collectives: 20.8 us -> 27.7 us  [round_trip(): lax.all_to_all(slot_block, 'attn', split_axis=0, concat_axis=0, tiled=True)]
    unnamed x3 -> x2, waiting for transfers between devices: 72 us -> 71.1 us
  transfers between devices with their start and end apart: 6 -> 9, of which waited for: 4 -> 7; matrix products, arithmetic and copies ran while one was open for 13% -> 16% of each run, Pallas kernels for 0% -> 0%
where the time goes in v1:
time: 324 us; the launch traced here: 323 us
  waiting for transfers between devices  99.3 us (31%)
  matrix products  71.7 us (22%)
  local copies, waits for them, and re-layouts  71.5 us (22%)
  starting transfers between devices  30.3 us (9%)
  blocking collectives  27.7 us (9%)
  between operations  13.6 us (4%)
  other arithmetic  9.13 us (3%)
    unnamed x2, waiting for transfers between devices  71.1 us
    unnamed x16, local copies, waits for them, and re-layouts  45.4 us
    dot_general x1, matrix products, local_attention(): jnp.dot(member_float.T, page_sum.reshape(pool_size, -1), precision=HIGHEST)  28.2 us
    all_to_all x1, blocking collectives, round_trip(): lax.all_to_all(slot_block, 'attn', split_axis=0, concat_axis=0, tiled=True)  27.7 us
    dot_general x1, matrix products, local_attention(): jnp.einsum('pht,ptc->phc', probs, cache[:, :, :latent_width], preferred_e...  17.2 us
    dot_general x1, matrix products, local_attention(): jnp.einsum('phc,ptc->pht', picked, cache, preferred_element_type=jnp.floa...  15.5 us
    ppermute x4, waiting for transfers between devices, on_device(): lax.ppermute(attn_out, 'expert', [(dev, dev ^ hop) for dev in range(16)])  14.9 us
    gather x1, local copies, waits for them, and re-layouts, local_attention(): picked = jnp.take(queries, safe_owner, axis=0)  10.3 us
  transfers between devices with their start and end apart: 9, of which 7 were waited for; matrix products, arithmetic and copies ran while one was open for 16% of the time, Pallas kernels for 0%

profile of v1, /device:TPU:1, one launch (start us, length us, event | category | flops | bytes accessed | tf_op | source)
XLA Modules:
  0.0 323.2 jit_solution(8656677637486394648)
XLA Ops:
  6.5 0.7 broadcast_minimum_fusion
  8.0 10.3 %gather_fusion = bf16[192,64,576]{2,1,0:T(8,128)(2,1)} fusion(bf16[4,64,576]{2,1,0:T(8,128)(2,1)} %param.11, s32[1024]{0:T(1024)S(1)} %pad_clamp_fusion), kind=kCustom, calls=%fused_computation | custom fusion | bytes 28312320 | tf_op jit(solution)/shard_map/jit(_take)/gather | solution.py:18
  18.3 15.5 %fusion.3 = f32[192,64,64]{1,2,0:T(8,128)} fusion(bf16[192,64,576]{2,1,0:T(8,128)(2,1)} %param.12, bf16[192,64,576]{2,1,0:T(8,128)(2,1)} %gather_fusion, pred[192]{0:T(512)(128)(4,1)S(1)} %get-tuple-element.14), kind=kOutput, calls=%fused_computation.5 | convolution fusion | flops 913047552 | bytes 31457472 | tf_op jit(solution)/shard_map/phc,ptc->pht/dot_general | solution.py:20
  33.7 7.6 %copy.80 = f32[192,64,64]{0,2,1:T(8,128)} copy(f32[192,64,64]{1,2,0:T(8,128)} %fusion.3) | data formatting | bytes 6291456 | tf_op jit(solution)/shard_map/phc,ptc->pht/dot_general | solution.py:20
  41.3 2.9 multiply_reduce_fusion
  45.5 3.5 %fusion.14 = (f32[192,64]{0,1:T(8,128)S(1)}, bf16[192,64,64]{0,2,1:T(8,128)(2,1)S(1)}) fusion(f32[192,64,64]{0,2,1:T(8,128)} %copy.80, f32[192,64]{0,1:T(8,128)S(1)} %copy.86, pred[192]{0:T(512)(128)(4,1)S(1)} %get-tuple-element.13), kind=kLoop, calls=%fused_computation.20 | loop fusion | flops 3919872 | bytes 4817088 | tf_op jit(solution)/shard_map/reduce_sum | solution.py:37
  49.0 0.8 fusion.42
  49.7 7.6 %all-to-all-start.2 = ((f32[1,4,64]{1,0,2:T(1,128)}), f32[1,4,64]{1,0,2:T(1,128)S(1)}, u32[]{:S(2)}, u32[]{:S(2)}) async-start(f32[1,4,64]{1,0,2:T(1,128)} %bitcast.38), calls=%async_computation.2 | async-start | bytes 65536 | tf_op jit(solution)/shard_map/all_to_all | solution.py:78
  57.3 3.8 %copy.87 = bf16[192,64,64]{2,1,0:T(8,128)(2,1)} copy(bf16[192,64,64]{0,2,1:T(8,128)(2,1)S(1)} %get-tuple-element.10) | data formatting | bytes 3145728 | tf_op jit(solution)/shard_map/convert_element_type | solution.py:32
  61.1 17.2 %fusion.6 = f32[192,64,512]{2,1,0:T(8,128)} fusion(bf16[192,64,64]{2,1,0:T(8,128)(2,1)} %copy.87, bf16[192,64,576]{2,1,0:T(8,128)(2,1)} %param.12), kind=kOutput, calls=%fused_computation.8 | convolution fusion | flops 805306368 | bytes 40894464 | tf_op jit(solution)/shard_map/pht,ptc->phc/dot_general | solution.py:33
  79.1 6.7 %all-to-all-start = ((f32[1,4,64]{1,0,2:T(1,128)}), f32[1,4,64]{1,0,2:T(1,128)S(1)}, u32[]{:S(2)}, u32[]{:S(2)}) async-start(f32[1,4,64]{1,0,2:T(1,128)} %copy.83), calls=%async_computation | async-start | bytes 65536 | tf_op jit(solution)/shard_map/all_to_all | solution.py:77
  85.7 28.2 %fusion.16 = f32[1,4,64,512]{3,1,0,2:T(4,128)} fusion(pred[192,4]{0,1:T(4,128)(4,1)S(1)} %fusion.37, f32[24,8,64,512]{3,2,1,0:T(8,128)} %bitcast.99), kind=kOutput, calls=%fused_computation.22 | convolution fusion | flops 301989888 | bytes 25690880 | tf_op jit(solution)/shard_map/dot_general | solution.py:38
  114.0 6.7 %all-to-all-start.1 = ((f32[1,4,64,512]{3,1,0,2:T(4,128)}), f32[1,4,64,512]{3,1,0,2:T(4,128)S(1)}, u32[]{:S(2)}, u32[]{:S(2)}) async-start(f32[1,4,64,512]{3,1,0,2:T(4,128)} %fusion.16), calls=%async_computation.1 | async-start | bytes 1048576 | tf_op jit(solution)/shard_map/all_to_all | solution.py:79
  121.7 8.2 %all-to-all-done.1 = f32[1,4,64,512]{3,1,0,2:T(4,128)S(1)} async-done(((f32[1,4,64,512]{3,1,0,2:T(4,128)}), f32[1,4,64,512]{3,1,0,2:T(4,128)S(1)}, u32[]{:S(2)}, u32[]{:S(2)}) %all-to-all-start.1) | async-done | bytes 524320 | tf_op jit(solution)/shard_map/all_to_all | solution.py:79
  130.1 4.3 %fusion.22 = f32[4,7168]{1,0:T(4,128)S(1)} fusion(bf16[512,7168]{1,0:T(8,128)(2,1)} %param.15, bf16[4,512,128]{2,1,0:T(8,128)(2,1)S(1)} %copy-done, f32[4,4,512]{2,0,1:T(4,128)S(1)} %multiply_reduce_fusion.1, f32[4,4]{0,1:T(4,128)S(1)} %copy.92), kind=kOutput, calls=%fused_computation.27 | convolution fusion | flops 31475712 | bytes 8011840 | tf_op jit(solution)/shard_map/dot_general | solution.py:91
  134.7 3.3 %collective-permute-done = f32[4,7168]{1,0:T(4,128)S(1)} collective-permute-done((f32[4,7168]{1,0:T(4,128)S(1)}, f32[4,7168]{1,0:T(4,128)S(1)}, u32[]{:S(2)}, u32[]{:S(2)}) %collective-permute-start) | collective-permute-done | bytes 114720 | tf_op jit(solution)/shard_map/ppermute | solution.py:94
  138.1 0.9 collective-permute-start.1
  139.1 4.2 %collective-permute-done.1 = f32[4,7168]{1,0:T(4,128)S(1)} collective-permute-done((f32[4,7168]{1,0:T(4,128)S(1)}, f32[4,7168]{1,0:T(4,128)S(1)}, u32[]{:S(2)}, u32[]{:S(2)}) %collective-permute-start.1) | collective-permute-done | bytes 114720 | tf_op jit(solution)/shard_map/ppermute | solution.py:94
  143.8 3.2 %collective-permute-done.2 = f32[4,7168]{1,0:T(4,128)S(1)} collective-permute-done((f32[4,7168]{1,0:T(4,128)S(1)}, f32[4,7168]{1,0:T(4,128)S(1)}, u32[]{:S(2)}, u32[]{:S(2)}) %collective-permute-start.2) | collective-permute-done | bytes 114720 | tf_op jit(solution)/shard_map/ppermute | solution.py:94
  147.1 1.1 collective-permute-start.3
  148.3 4.1 %collective-permute-done.3 = f32[4,7168]{1,0:T(4,128)S(1)} collective-permute-done((f32[4,7168]{1,0:T(4,128)S(1)}, f32[4,7168]{1,0:T(4,128)S(1)}, u32[]{:S(2)}, u32[]{:S(2)}) %collective-permute-start.3) | collective-permute-done | bytes 114720 | tf_op jit(solution)/shard_map/ppermute | solution.py:94
  153.3 27.7 %all_to_all.64 = bf16[8,2,4,7168]{3,2,1,0:T(4,128)(2,1)S(1)} all-to-all(bf16[8,2,4,7168]{3,2,1,0:T(4,128)(2,1)S(1)} %reshape.116), channel_id=1, replica_groups=mesh['attn'=8,'expert'=16] {'attn'}, dimensions={0} | all-to-all | bytes 1835008 | tf_op jit(solution)/shard_map/all_to_all | solution.py:52
  181.0 3.0 fusion.10
  184.1 0.8 fusion.12
  185.5 18.9 %copy.103 = f32[8,2,4,7168]{0,2,1,3:T(4,128)} copy(f32[8,2,4,7168]{3,0,2,1:T(8,128)S(1)} %convolution_bitcast_fusion) | data formatting | bytes 3670016
  204.4 24.2 %reshape.140 = f32[7168,64]{1,0:T(8,128)} reshape(f32[7168,2,4,8]{3,2,1,0:T(4,128)} %bitcast.100) | data formatting | bytes 3670016
  228.7 71.1 %reduce-scatter.4.cloned.1.call-done = f32[448,64]{1,0:T(8,128)} async-done(((f32[7168,64]{1,0:T(8,128)}), f32[448,64]{1,0:T(8,128)}) %reduce-scatter.4.cloned.1.call-update) | async-done | bytes 114704
  299.8 2.2 reshape.141
  301.9 1.6 copy.97
  303.5 6.8 %all-to-all-start.4 = ((f32[8,2,4,448]{3,2,1,0:T(4,128)}), f32[8,2,4,448]{3,2,1,0:T(4,128)S(1)}, u32[]{:S(2)}, u32[]{:S(2)}) async-start(f32[8,2,4,448]{3,2,1,0:T(4,128)} %copy.97), calls=%async_computation.4 | async-start | bytes 262144 | tf_op jit(solution)/shard_map/all_to_all | solution.py:55
  310.4 5.2 %all-to-all-done.4 = f32[8,2,4,448]{3,2,1,0:T(4,128)S(1)} async-done(((f32[8,2,4,448]{3,2,1,0:T(4,128)}), f32[8,2,4,448]{3,2,1,0:T(4,128)S(1)}, u32[]{:S(2)}, u32[]{:S(2)}) %all-to-all-start.4) | async-done | bytes 114720 | tf_op jit(solution)/shard_map/all_to_all | solution.py:55
  315.6 0.8 add_convert_fusion
  (53 shorter events, 6.7 us)
Async XLA Ops:
  6.5 123.5 %copy-start = (bf16[4,512,128]{2,1,0:T(8,128)(2,1)S(1)}, bf16[4,512,128]{2,1,0:T(8,128)(2,1)}, u32[]{:S(2)}) copy-start(bf16[4,512,128]{2,1,0:T(8,128)(2,1)} %param.14) | copy-start | bytes 1572868
  49.7 29.3 %all-to-all-start.2 = ((f32[1,4,64]{1,0,2:T(1,128)}), f32[1,4,64]{1,0,2:T(1,128)S(1)}, u32[]{:S(2)}, u32[]{:S(2)}) async-start(f32[1,4,64]{1,0,2:T(1,128)} %bitcast.38), calls=%async_computation.2 | async-start | bytes 65536 | tf_op jit(solution)/shard_map/all_to_all | solution.py:78
  79.1 34.9 %all-to-all-start = ((f32[1,4,64]{1,0,2:T(1,128)}), f32[1,4,64]{1,0,2:T(1,128)S(1)}, u32[]{:S(2)}, u32[]{:S(2)}) async-start(f32[1,4,64]{1,0,2:T(1,128)} %copy.83), calls=%async_computation | async-start | bytes 65536 | tf_op jit(solution)/shard_map/all_to_all | solution.py:77
  114.0 15.9 %all-to-all-start.1 = ((f32[1,4,64,512]{3,1,0,2:T(4,128)}), f32[1,4,64,512]{3,1,0,2:T(4,128)S(1)}, u32[]{:S(2)}, u32[]{:S(2)}) async-start(f32[1,4,64,512]{3,1,0,2:T(4,128)} %fusion.16), calls=%async_computation.1 | async-start | bytes 1048576 | tf_op jit(solution)/shard_map/all_to_all | solution.py:79
  120.7 179.1 %reduce-scatter.4.cloned.1.call-start = ((), (), s32[]{:S(2)}) async-start(), calls=%async_computation.6 | async-start | bytes 3899392
  130.1 8.9 %copy-start.3 = (s32[4,8]{1,0:T(4,128)S(1)}, s32[4,8]{1,0:T(4,128)}, u32[]{:S(2)}) copy-start(s32[4,8]{1,0:T(4,128)} %param.17) | copy-start | bytes 388
  130.1 22.4 %copy-start.2 = (f32[7168]{0:T(1024)S(1)}, f32[7168]{0:T(1024)}, u32[]{:S(2)}) copy-start(f32[7168]{0:T(1024)} %param.16) | copy-start | bytes 86020
  134.4 3.6 %collective-permute-start = (f32[4,7168]{1,0:T(4,128)S(1)}, f32[4,7168]{1,0:T(4,128)S(1)}, u32[]{:S(2)}, u32[]{:S(2)}) collective-permute-start(f32[4,7168]{1,0:T(4,128)S(1)} %fusion.22), channel_id=1, source_target_pairs={{0,1},{1,0},{2,3},{3,2},{4,5},{5,4},{6,7},{7,6},{8,9},{9,8},{10,11... | collective-permute-start | bytes 344072 | tf_op jit(solution)/shard_map/ppermute | solution.py:94
  138.1 5.2 %collective-permute-start.1 = (f32[4,7168]{1,0:T(4,128)S(1)}, f32[4,7168]{1,0:T(4,128)S(1)}, u32[]{:S(2)}, u32[]{:S(2)}) collective-permute-start(f32[4,7168]{1,0:T(4,128)S(1)} %add.48), channel_id=1, source_target_pairs={{0,2},{1,3},{2,0},{3,1},{4,6},{5,7},{6,4},{7,5},{8,10},{9,11},{10,... | collective-permute-start | bytes 344072 | tf_op jit(solution)/shard_map/ppermute | solution.py:94
  143.4 3.7 %collective-permute-start.2 = (f32[4,7168]{1,0:T(4,128)S(1)}, f32[4,7168]{1,0:T(4,128)S(1)}, u32[]{:S(2)}, u32[]{:S(2)}) collective-permute-start(f32[4,7168]{1,0:T(4,128)S(1)} %add.49), channel_id=1, source_target_pairs={{0,4},{1,5},{2,6},{3,7},{4,0},{5,1},{6,2},{7,3},{8,12},{9,13},{10,... | collective-permute-start | bytes 344072 | tf_op jit(solution)/shard_map/ppermute | solution.py:94
  147.1 5.2 %collective-permute-start.3 = (f32[4,7168]{1,0:T(4,128)S(1)}, f32[4,7168]{1,0:T(4,128)S(1)}, u32[]{:S(2)}, u32[]{:S(2)}) collective-permute-start(f32[4,7168]{1,0:T(4,128)S(1)} %add.50), channel_id=1, source_target_pairs={{0,8},{1,9},{2,10},{3,11},{4,12},{5,13},{6,14},{7,15},{8,0},{9,1},... | collective-permute-start | bytes 344072 | tf_op jit(solution)/shard_map/ppermute | solution.py:94
  153.3 30.7 %copy-start.5 = (bf16[2,7168,128]{2,1,0:T(8,128)(2,1)S(1)}, bf16[2,7168,128]{2,1,0:T(8,128)(2,1)}, u32[]{:S(2)}) copy-start(bf16[2,7168,128]{2,1,0:T(8,128)(2,1)} %param.19) | copy-start | bytes 11010052
  181.0 3.8 %copy-start.1 = (bf16[2,128,7168]{2,1,0:T(8,128)(2,1)S(1)}, bf16[2,128,7168]{2,1,0:T(8,128)(2,1)}, u32[]{:S(2)}) copy-start(bf16[2,128,7168]{2,1,0:T(8,128)(2,1)} %param.21) | copy-start | bytes 11010052
  228.6 81.7 %copy-start.4 = (f32[4,8]{1,0:T(4,128)S(1)}, f32[4,8]{1,0:T(4,128)}, u32[]{:S(2)}) copy-start(f32[4,8]{1,0:T(4,128)} %param.18) | copy-start | bytes 388
  303.5 12.1 %all-to-all-start.4 = ((f32[8,2,4,448]{3,2,1,0:T(4,128)}), f32[8,2,4,448]{3,2,1,0:T(4,128)S(1)}, u32[]{:S(2)}, u32[]{:S(2)}) async-start(f32[8,2,4,448]{3,2,1,0:T(4,128)} %copy.97), calls=%async_computation.4 | async-start | bytes 262144 | tf_op jit(solution)/shard_map/all_to_all | solution.py:55
Sparse Core Ops, SparseCore 0:
  228.8 70.9 reduce-scatter.3
